TPU v7x, 32 devices: a whole 2x2x4 slice. The times are simulated.
32 devices in a mesh: gy: 4 (over y, core), gz: 8 (over z, x).
Axes of the slice: x: 2, y: 2, z: 4, core: 2. Of those that a mesh axis runs over, the one named last changes fastest.
Arguments:
- offset: float32 [3, 65536], P(None, ('gy', 'gz')), may hold values from 0.6 to 1.4
- velocity: float32 [3, 65536], P(None, ('gy', 'gz')), may hold values from -4 to 4
- affine: float32 [9, 65536], P(None, ('gy', 'gz')), may hold values from -3 to 3
- deform: float32 [9, 65536], P(None, ('gy', 'gz')), as said below
- cell_index: int32 [65536], P(('gy', 'gz')), may hold values from 1 to 16382, as said below
- live_count: int32 [32], P(('gy', 'gz')), may hold values from 128 to 2048, as said below
- grip_mask: int32 [64, 64, 128], P('gy', 'gz'), may hold values from 0 to 2
- grip_velocity: float32 [2, 2, 3], replicated, may hold values from -4 to 4
- loss_offset: float32 [3, 65536], P(None, ('gy', 'gz')), may hold values from -6 to 6
- loss_velocity: float32 [3, 65536], P(None, ('gy', 'gz')), may hold values from -6 to 6
- loss_affine: float32 [9, 65536], P(None, ('gy', 'gz')), may hold values from -6 to 6
- loss_deform: float32 [9, 65536], P(None, ('gy', 'gz')), may hold values from -6 to 6
Outputs:
- grad_offset: float32 [3, 65536], P(None, ('gy', 'gz'))
- grad_velocity: float32 [3, 65536], P(None, ('gy', 'gz'))
- grad_affine: float32 [9, 65536], P(None, ('gy', 'gz'))
- grad_deform: float32 [9, 65536], P(None, ('gy', 'gz'))
- grad_grip: float32 [2, 2, 3], replicated
Inputs may be any that keep to these rules, and one draw needn't show every extreme that they name: cell_index % 128 lies between 1 and 126. `live_count`: a multiple of 128. `deform`: every row's determinant is at least 0.5.
All inputs are finite; a program needn't handle non-finite values.
Results may differ from a plain program's by a relative error of at most 0.0001.
Values sent between devices are 32-bit elements; how exact they have to be, the bound alone decides.
A program may use at most 192 MiB of HBM per device.

v0:
```python
import functools

import jax
import jax.numpy as jnp
from jax import lax
from jax.experimental import pallas as pl
from jax.experimental.pallas import tpu as pltpu
from jax.sharding import PartitionSpec as P

DT = 0.05
SHEAR = 10.0
BULK = 10.0
GRAVITY = -2.0
MASS_REG = 0.1
F32 = jnp.float32
BF16 = jnp.bfloat16
MESH = pl.DeviceIdType.MESH
DIRS = [(-1, -1), (-1, 0), (-1, 1), (0, -1), (0, 1), (1, -1), (1, 0), (1, 1)]
YB = 4
COMPS = (5, 4, 3, 3)


def splines(f):
    return (0.5 * (1.5 - f) ** 2, 0.75 - (f - 1.0) ** 2, 0.5 * (f - 0.5) ** 2)


def dsplines(f):
    return (f - 1.5, -2.0 * (f - 1.0), f - 0.5)


def pick3(b, vals):
    return jnp.where(b == 0, vals[0], jnp.where(b == 1, vals[1], jnp.where(b == 2, vals[2], 0.0)))


def sub_sum(x):
    return jnp.sum(x, axis=0, keepdims=True)


def split(x):
    hi = x.astype(BF16)
    lo = (x - hi.astype(F32)).astype(BF16)
    return hi, lo


def stress(c_rows, f_rows):
    f = f_rows
    cof = [
        f[4] * f[8] - f[5] * f[7],
        f[5] * f[6] - f[3] * f[8],
        f[3] * f[7] - f[4] * f[6],
        f[2] * f[7] - f[1] * f[8],
        f[0] * f[8] - f[2] * f[6],
        f[1] * f[6] - f[0] * f[7],
        f[1] * f[5] - f[2] * f[4],
        f[2] * f[3] - f[0] * f[5],
        f[0] * f[4] - f[1] * f[3],
    ]
    det = f[0] * cof[0] + f[1] * cof[1] + f[2] * cof[2]
    log_det = jnp.log(det)
    a_rows = []
    for i in range(3):
        for j in range(3):
            left = f[3 * i] * f[3 * j] + f[3 * i + 1] * f[3 * j + 1] + f[3 * i + 2] * f[3 * j + 2]
            tau = SHEAR * (left - 1.0) + BULK * log_det if i == j else SHEAR * left
            a_rows.append(c_rows[3 * i + j] - 4.0 * DT * tau)
    return a_rows, det, cof


def kernel(
    ny, nz, span_y, span_z, span_x, rows, chunk,
    off_ref, vel_ref, aff_ref, def_ref, idx_ref, live_ref, mask_ref, grip_ref,
    lo_ref, lv_ref, la_ref, ld_ref,
    go_ref, gv_ref, ga_ref, gd_ref, gg_ref,
    oh, oht, acc, grid, ybuf, sums, maskx, u_hi, u_lo, node, node_b,
    off1, vel1, aff1, def1, aff2, vel2, up_o, up_v, up_a, up_d,
    rz, ry, rc, gsend, gbuf1, gsend2, gbuf2,
    send_sem, recv_sem, gs1, gr1, gs2, gr2,
):
    me_y = lax.axis_index("gy")
    me_z = lax.axis_index("gz")
    zr = span_z + 2
    bands = span_y // YB
    yp = grid.shape[2]
    zbits = span_z.bit_length() - 1
    xbits = span_x.bit_length() - 1
    steps = rows // chunk

    barrier = pltpu.get_barrier_semaphore()

    @pl.loop(1, nz)
    def _(d):
        pl.semaphore_signal(barrier, inc=1, device_id=(me_y, lax.rem(me_z + d, nz)), device_id_type=MESH)

    @pl.loop(1, ny)
    def _(d):
        pl.semaphore_signal(barrier, inc=1, device_id=(lax.rem(me_y + d, ny), me_z), device_id_type=MESH)

    def exists(d):
        dy, dz = DIRS[d]
        ok = None
        if dy:
            ok = me_y > 0 if dy < 0 else me_y < ny - 1
        if dz:
            okz = me_z > 0 if dz < 0 else me_z < nz - 1
            ok = okz if ok is None else jnp.logical_and(ok, okz)
        return ok

    for d in (0, 2, 5, 7):
        @pl.when(exists(d))
        def _():
            pl.semaphore_signal(
                barrier, inc=1, device_id=(me_y + DIRS[d][0], me_z + DIRS[d][1]), device_id_type=MESH
            )

    def barrier_wait():
        sides_y = (me_y > 0).astype(jnp.int32) + (me_y < ny - 1).astype(jnp.int32)
        sides_z = (me_z > 0).astype(jnp.int32) + (me_z < nz - 1).astype(jnp.int32)
        pl.semaphore_wait(barrier, ny + nz - 2 + sides_y * sides_z)

    def column(sl):
        idx = idx_ref[:, sl]
        rem = idx >> xbits
        return ((rem >> (zbits + 2)) << xbits) + (idx & (span_x - 1))

    @pl.loop(0, steps)
    def _(s):
        sl = pl.ds(pl.multiple_of(s * chunk, chunk), chunk)
        col = column(sl)
        wide = bands * span_x
        rows_iota = lax.broadcasted_iota(jnp.int32, (wide, chunk), 0)
        oh[:, sl] = jnp.where(rows_iota == col, 1.0, 0.0).astype(BF16)
        col_t = jnp.transpose(jnp.broadcast_to(col.astype(F32), (128, chunk)))
        lane = lax.broadcasted_iota(jnp.int32, (chunk, 128), 1)
        for part in range(wide // 128):
            oht[sl, part * 128:(part + 1) * 128] = jnp.where(
                col_t == (lane + part * 128).astype(F32), 1.0, 0.0
            ).astype(BF16)

    def geometry(sl):
        rem = idx_ref[:, sl] >> xbits
        pz = rem & (span_z - 1)
        yl = (rem >> zbits) & (YB - 1)
        b = lax.broadcasted_iota(jnp.int32, (8, chunk), 0) - yl
        return pz, b

    def live_of(s):
        lane = lax.broadcasted_iota(jnp.int32, (1, chunk), 1) + s * chunk
        return jnp.where(lane < live_ref[0], 1.0, 0.0)

    def row_list(ref, sl):
        return [ref[i:i + 1, sl] for i in range(ref.shape[0])]

    def scatter_chunk(s, sl, f, v, a_mat, scale, mass):
        pz, b = geometry(sl)
        wx = splines(f[0])
        ex = [k - f[0] for k in range(3)]
        wy = pick3(b, splines(f[1]))
        if scale is not None:
            wy = wy * scale
        ey = b.astype(F32) - f[1]
        sz = splines(f[2])
        c = [z - pz for z in range(zr)]
        wyz = [wy * pick3(c[z], sz) for z in range(zr)]
        ez = [c[z].astype(F32) - f[2] for z in range(zr)]
        his, los = [], []
        for i in range(3):
            vy = v[i] + a_mat[3 * i + 1] * ey
            t = [wyz[z] * (vy + a_mat[3 * i + 2] * ez[z]) for z in range(zr)]
            for a in range(3):
                coef = wx[a] * (a_mat[3 * i] * ex[a])
                block = jnp.concatenate([t[z] * wx[a] + wyz[z] * coef for z in range(zr)], axis=0)
                hi, lo = split(block)
                his.append(hi)
                los.append(lo)
        if mass:
            for a in range(3):
                block = jnp.concatenate([wyz[z] * wx[a] for z in range(zr)], axis=0)
                hi, lo = split(block)
                his.append(hi)
                los.append(lo)
        hot = oht[sl, :]
        for i in range(4 if mass else 3):
            hi = jnp.concatenate(his[3 * i:3 * i + 3], axis=0)
            lo = jnp.concatenate(los[3 * i:3 * i + 3], axis=0)
            part = jnp.dot(hi, hot, preferred_element_type=F32)
            part = part + jnp.dot(lo, hot, preferred_element_type=F32)
            height = 3 * zr * 8
            acc[i * height:(i + 1) * height, :] += part

    def fold(comps):
        for i in range(comps):
            bands_out = []
            for h in range(bands):
                total = None
                for a in range(3):
                    at = (3 * i + a) * zr * 8
                    piece = acc[at:at + zr * 8, h * span_x:(h + 1) * span_x]
                    if a != 1:
                        piece = pltpu.roll(piece, (a - 1) % span_x, 1)
                    total = piece if total is None else total + piece
                bands_out.append(total.reshape(zr, 8, span_x))
            for h in range(0, bands, 2):
                grid[i, :, h * YB:h * YB + 8, :] = bands_out[h]
            grid[i, :, bands * YB:, :] = jnp.zeros((zr, yp - bands * YB, span_x), F32)
            for h in range(1, bands, 2):
                grid[i, :, h * YB:h * YB + 8, :] += bands_out[h]

    def slab(d, n):
        dy, dz = DIRS[d]
        zs = pl.ds(0, 2) if dz < 0 else pl.ds(zr - 2, 2)
        side = 0 if dy < 0 else 1
        if dy == 0:
            return grid.at[pl.ds(0, n), zs]
        if dz == 0:
            return ybuf.at[side, pl.ds(0, n)]
        return ybuf.at[side, pl.ds(0, n), zs]

    def landing(e, d, n):
        dy, dz = DIRS[d]
        if dy == 0:
            return rz.at[e, 0 if dz < 0 else 1, pl.ds(0, n)]
        if dz == 0:
            return ry.at[e, 0 if dy < 0 else 1, pl.ds(0, n)]
        return rc.at[e, (0 if dy < 0 else 2) + (0 if dz < 0 else 1), pl.ds(0, n)]

    def exchange(e, out):
        n = COMPS[e]
        ybuf[0, 0:n] = grid[0:n, :, 0:2, :]
        ybuf[1, 0:n] = grid[0:n, :, span_y:span_y + 2, :]
        order = (3, 4, 1, 6, 0, 2, 5, 7)
        for d in order:
            @pl.when(exists(d))
            def _():
                pltpu.make_async_remote_copy(
                    src_ref=slab(d, n), dst_ref=landing(e, 7 - d, n),
                    send_sem=send_sem.at[e, d], recv_sem=recv_sem.at[e, 7 - d],
                    device_id=(me_y + DIRS[d][0], me_z + DIRS[d][1]), device_id_type=MESH,
                ).start()
        for i in range(n):
            out(i)[...] = grid[i]
        for d in order:
            dy, dz = DIRS[d]

            @pl.when(exists(d))
            def _():
                copy = pltpu.make_async_remote_copy(
                    src_ref=slab(d, n), dst_ref=landing(e, d, n),
                    send_sem=send_sem.at[e, d], recv_sem=recv_sem.at[e, d],
                    device_id=(me_y + dy, me_z + dz), device_id_type=MESH,
                )
                copy.wait_recv()
                zs = slice(0, zr) if dz == 0 else (slice(0, 2) if dz < 0 else slice(zr - 2, zr))
                ys = slice(0, yp) if dy == 0 else (slice(0, 2) if dy < 0 else slice(span_y, span_y + 2))
                landed = landing(e, d, n)
                for i in range(n):
                    out(i)[zs, ys, :] += landed[i]
                copy.wait_send()

    def cell_kinds():
        shape = (zr, yp, span_x)
        gy = lax.broadcasted_iota(jnp.int32, shape, 1) - 1 + me_y * span_y
        gz = lax.broadcasted_iota(jnp.int32, shape, 0) - 1 + me_z * span_z
        sticky = (gy < 3) | (gy >= ny * span_y - 3) | (gz < 3) | (gz >= nz * span_z - 3)
        return sticky, maskx[...]

    def put_u(i, value):
        for a in range(3):
            turned = value.reshape(zr * yp, span_x)
            if a != 1:
                turned = pltpu.roll(turned, (1 - a) % span_x, 1)
            turned = turned.reshape(zr, yp, span_x)
            at = (3 * i + a) * zr * 8
            for h in range(bands):
                hi, lo = split(turned[:, h * YB:h * YB + 8, :].reshape(zr * 8, span_x))
                u_hi[at:at + zr * 8, h * span_x:(h + 1) * span_x] = hi
                u_lo[at:at + zr * 8, h * span_x:(h + 1) * span_x] = lo

    def settle(e):
        sticky, kind = cell_kinds()
        inv = 1.0 / (sums[e, 3] + MASS_REG)
        for i in range(3):
            u = sums[e, i] * inv
            if i == 1:
                u = u + DT * GRAVITY
            u = jnp.where(sticky, 0.0, u)
            for k in range(2):
                u = jnp.where(kind == float(k + 1), grip_ref[(e * 2 + k) * 3 + i], u)
            put_u(i, u)

    def settle_back(e):
        sticky, kind = cell_kinds()
        free = jnp.logical_and(jnp.logical_not(sticky), kind == 0.0)
        inv = 1.0 / (sums[e, 3] + MASS_REG)
        mass = None
        for i in range(3):
            gu = sums[2, i]
            for k in range(2):
                hit = jnp.where(kind == float(k + 1), gu, 0.0)
                part = jnp.sum(hit[1:span_z + 1], axis=0)
                part = sub_sum(part[1:span_y + 1])
                gsend[e, 3 * k + i:3 * k + i + 1, :] = part
            gs = jnp.where(free, gu * inv, 0.0)
            term = gs * sums[e, i]
            mass = term if mass is None else mass + term
            put_u(i, gs)
        put_u(3, -mass * inv)

    def gather_chunk(sl, comps):
        pz, b = geometry(sl)
        hot = oh[:, sl]
        bits = [(pz & (1 << k)) != 0 for k in range(zbits)]
        out = []
        for i in range(comps):
            for a in range(3):
                at = (3 * i + a) * zr * 8
                h = jnp.dot(u_hi[at:at + zr * 8, :], hot, preferred_element_type=F32)
                h = h + jnp.dot(u_lo[at:at + zr * 8, :], hot, preferred_element_type=F32)
                vals = [h[z * 8:(z + 1) * 8] for z in range(zr)]
                for k in reversed(range(zbits)):
                    shift = 1 << k
                    vals = [
                        jnp.where(bits[k], vals[z + shift], vals[z]) for z in range(len(vals) - shift)
                    ]
                out.append(vals)
        return out

    def moments(vals, f, b):
        wx = splines(f[0])
        wz = splines(f[2])
        wex = [wx[a] * (a - f[0]) for a in range(3)]
        wez = [wz[c] * (c - f[2]) for c in range(3)]
        wy = pick3(b, splines(f[1]))
        wey = wy * (b.astype(F32) - f[1])
        plain, first = [], []
        for i in range(3):
            x0 = [sum(wx[a] * vals[3 * i + a][c] for a in range(3)) for c in range(3)]
            x1 = [sum(wex[a] * vals[3 * i + a][c] for a in range(3)) for c in range(3)]
            z00 = sum(wz[c] * x0[c] for c in range(3))
            z10 = sum(wz[c] * x1[c] for c in range(3))
            z01 = sum(wez[c] * x0[c] for c in range(3))
            plain.append(sub_sum(wy * z00))
            first += [sub_sum(wy * z10), sub_sum(wey * z00), sub_sum(wy * z01)]
        return plain, first

    def weight_pull(vals, f, b, g, d_mat, extra):
        wx, dx = splines(f[0]), dsplines(f[0])
        wz, dz = splines(f[2]), dsplines(f[2])
        wy = pick3(b, splines(f[1]))
        dy = pick3(b, dsplines(f[1]))
        ey = b.astype(F32) - f[1]
        k_rows = [g[i] + d_mat[3 * i + 1] * ey for i in range(3)]
        by_x = [[d_mat[3 * i] * (a - f[0]) for a in range(3)] for i in range(3)]
        by_z = [[d_mat[3 * i + 2] * (c - f[2]) for c in range(3)] for i in range(3)]
        s_x = s_y = s_z = 0.0
        for c in range(3):
            q_w = q_d = 0.0
            for a in range(3):
                q = sum(vals[3 * i + a][c] * (k_rows[i] + (by_x[i][a] + by_z[i][c])) for i in range(3))
                if extra:
                    q = q + vals[9 + a][c]
                q_w = q_w + wx[a] * q
                q_d = q_d + dx[a] * q
            s_x = s_x + wz[c] * q_d
            s_y = s_y + wz[c] * q_w
            s_z = s_z + dz[c] * q_w
        return [sub_sum(wy * s_x), sub_sum(dy * s_y), sub_sum(wy * s_z)]

    states = ((off_ref, vel_ref, aff_ref, def_ref), (off1, vel1, aff1, def1))
    afters = ((off1, vel1, aff1, def1), (None, vel2, aff2, None))

    def forward(e):
        o_r, v_r, a_r, d_r = states[e]
        acc[...] = jnp.zeros_like(acc)

        @pl.loop(0, steps)
        def _(s):
            sl = pl.ds(pl.multiple_of(s * chunk, chunk), chunk)
            a_mat, _, _ = stress(row_list(a_r, sl), row_list(d_r, sl))
            scatter_chunk(s, sl, row_list(o_r, sl), row_list(v_r, sl), a_mat, live_of(s), True)

        fold(4)
        if e == 0:
            grid[4] = jnp.zeros((zr, yp, span_x), F32)
            for z in range(span_z):
                grid[4, z + 1, 1:span_y + 1, :] = mask_ref[:, z, :].astype(F32)
            barrier_wait()
        exchange(e, lambda i: sums.at[e, i] if i < 4 else maskx)
        settle(e)
        n_o, n_v, n_a, n_d = afters[e]

        @pl.loop(0, steps)
        def _(s):
            sl = pl.ds(pl.multiple_of(s * chunk, chunk), chunk)
            _, b = geometry(sl)
            f = row_list(o_r, sl)
            vals = gather_chunk(sl, 3)
            for r in range(9):
                for c in range(3):
                    node[e, 3 * r + c, :, sl] = vals[r][c]
            plain, first = moments(vals, f, b)
            new_a = [4.0 * m for m in first]
            for i in range(3):
                n_v[i:i + 1, sl] = plain[i]
            for i in range(9):
                n_a[i:i + 1, sl] = new_a[i]
            if n_o is not None:
                dm = row_list(d_r, sl)
                for i in range(3):
                    n_o[i:i + 1, sl] = f[i] + DT * plain[i]
                for i in range(3):
                    for k in range(3):
                        n_d[3 * i + k:3 * i + k + 1, sl] = dm[3 * i + k] + DT * sum(
                            new_a[3 * i + j] * dm[3 * j + k] for j in range(3)
                        )

    def gather_seeds(e, s, sl, dm):
        if e == 1:
            live = live_of(s)
            up = [[live * r for r in row_list(ref, sl)] for ref in (lo_ref, lv_ref, la_ref, ld_ref)]
        else:
            up = [row_list(ref, sl) for ref in (up_o, up_v, up_a, up_d)]
        g_o, g_v, g_a, g_d = up
        g = [g_v[i] + DT * g_o[i] for i in range(3)]
        d_mat = [
            4.0 * (g_a[3 * i + j] + DT * sum(g_d[3 * i + k] * dm[3 * j + k] for k in range(3)))
            for i in range(3)
            for j in range(3)
        ]
        return g_o, g_d, g, d_mat

    def backward(e, before, between):
        o_r, v_r, a_r, d_r = states[e]
        n_v, n_a = afters[e][1], afters[e][2]
        acc[...] = jnp.zeros_like(acc)

        @pl.loop(0, steps)
        def _(s):
            sl = pl.ds(pl.multiple_of(s * chunk, chunk), chunk)
            _, _, g, d_mat = gather_seeds(e, s, sl, row_list(d_r, sl))
            scatter_chunk(s, sl, row_list(o_r, sl), g, d_mat, None, False)

        fold(3)
        exchange(3 - e, lambda i: sums.at[2, i])
        settle_back(e)
        before()
        outs = (up_o, up_v, up_a, up_d) if e == 1 else (go_ref, gv_ref, ga_ref, gd_ref)

        def body(s):
            sl = pl.ds(pl.multiple_of(s * chunk, chunk), chunk)
            _, b = geometry(sl)
            live = live_of(s)
            f = row_list(o_r, sl)
            dm = row_list(d_r, sl)
            g_o, g_d, g, d_mat = gather_seeds(e, s, sl, dm)
            held = [[node[e, 3 * r + c, :, sl] for c in range(3)] for r in range(9)]
            pull = weight_pull(held, f, b, g, d_mat, False)
            vn = row_list(n_v, sl)
            cn = row_list(n_a, sl)
            grad_o = [
                g_o[k] + pull[k] - sum(d_mat[3 * i + k] * vn[i] for i in range(3)) for k in range(3)
            ]
            grad_d = [
                g_d[3 * j + k] + DT * sum(cn[3 * i + j] * g_d[3 * i + k] for i in range(3))
                for j in range(3)
                for k in range(3)
            ]
            vals = gather_chunk(sl, 4)
            plain, first = moments(vals, f, b)
            grad_v = [live * m for m in plain]
            grad_a = [live * m for m in first]
            a_mat, det, cof = stress(row_list(a_r, sl), dm)
            pull = weight_pull(vals, f, b, row_list(v_r, sl), a_mat, True)
            for k in range(3):
                outs[0][k:k + 1, sl] = grad_o[k] + live * pull[k] - sum(
                    a_mat[3 * i + k] * grad_v[i] for i in range(3)
                )
                outs[1][k:k + 1, sl] = grad_v[k]
            scale = (-4.0 * DT * BULK) * (grad_a[0] + grad_a[4] + grad_a[8]) / det
            for i in range(3):
                for k in range(3):
                    sym = sum((grad_a[3 * i + j] + grad_a[3 * j + i]) * dm[3 * j + k] for j in range(3))
                    at = 3 * i + k
                    outs[2][at:at + 1, sl] = grad_a[at]
                    outs[3][at:at + 1, sl] = grad_d[at] + (-4.0 * DT * SHEAR) * sym + scale * cof[at]

        pl.loop(0, steps // 2)(body)
        between()
        pl.loop(steps // 2, steps)(body)

    def grip_copy(axis, n, me, peer, slot, src, buf, ssem, rsem):
        device = (me_y, peer) if axis == "gz" else (peer, me_z)
        return pltpu.make_async_remote_copy(
            src_ref=src, dst_ref=buf.at[slot], send_sem=ssem.at[peer], recv_sem=rsem.at[slot],
            device_id=device, device_id_type=MESH,
        )

    def grip_start(axis, n, me, src, buf, ssem, rsem):
        buf[pl.ds(me, 1)] = src[...][None]

        @pl.loop(1, n)
        def _(d):
            grip_copy(axis, n, me, lax.rem(me + d, n), me, src, buf, ssem, rsem).start()

    def grip_finish(axis, n, me, src, buf, ssem, rsem):
        @pl.loop(1, n)
        def _(d):
            peer = lax.rem(me + d, n)
            copy = grip_copy(axis, n, me, peer, peer, src, buf, ssem, rsem)
            copy.wait_recv()
            copy.wait_send()

        total = buf[0]
        for at in range(1, n):
            total = total + buf[at]
        return total

    stage1 = ("gz", nz, me_z, gsend, gbuf1, gs1, gr1)
    stage2 = ("gy", ny, me_y, gsend2, gbuf2, gs2, gr2)

    def between_last():
        gsend2[...] = grip_finish(*stage1)
        grip_start(*stage2)

    def nothing():
        return None

    gsend[...] = jnp.zeros_like(gsend)
    forward(0)
    forward(1)
    backward(1, nothing, nothing)
    backward(0, lambda: grip_start(*stage1), between_last)
    total = grip_finish(*stage2)
    gg_ref[...] = jnp.broadcast_to(jnp.sum(total, axis=2, keepdims=True), total.shape)


def shards(ny, nz, offset, velocity, affine, deform, cell_index, live_count, grip_mask, grip_velocity,
           loss_offset, loss_velocity, loss_affine, loss_deform):
    span_y, span_z, span_x = grip_mask.shape
    rows = offset.shape[1]
    chunk = 256
    zr = span_z + 2
    bands = span_y // YB
    yp = (span_y + 2 + 7) // 8 * 8
    wide = bands * span_x
    vmem = pl.BlockSpec(memory_space=pltpu.VMEM)
    smem = pl.BlockSpec(memory_space=pltpu.SMEM)
    shape = jax.ShapeDtypeStruct
    scratch = [
        pltpu.VMEM((wide, rows), BF16),
        pltpu.VMEM((rows, wide), BF16),
        pltpu.VMEM((12 * zr * 8, wide), F32),
        pltpu.VMEM((5, zr, yp, span_x), F32),
        pltpu.VMEM((2, 5, zr, 2, span_x), F32),
        pltpu.VMEM((3, 4, zr, yp, span_x), F32),
        pltpu.VMEM((zr, yp, span_x), F32),
        pltpu.VMEM((12 * zr * 8, wide), BF16),
        pltpu.VMEM((12 * zr * 8, wide), BF16),
        pltpu.VMEM((2, 27, 8, rows), F32),
        pltpu.VMEM((8, 128), F32),
        pltpu.VMEM((3, rows), F32),
        pltpu.VMEM((3, rows), F32),
        pltpu.VMEM((9, rows), F32),
        pltpu.VMEM((9, rows), F32),
        pltpu.VMEM((9, rows), F32),
        pltpu.VMEM((3, rows), F32),
        pltpu.VMEM((3, rows), F32),
        pltpu.VMEM((3, rows), F32),
        pltpu.VMEM((9, rows), F32),
        pltpu.VMEM((9, rows), F32),
        pltpu.VMEM((4, 2, 5, 2, yp, span_x), F32),
        pltpu.VMEM((4, 2, 5, zr, 2, span_x), F32),
        pltpu.VMEM((4, 4, 5, 2, 2, span_x), F32),
        pltpu.VMEM((2, 8, span_x), F32),
        pltpu.VMEM((nz, 2, 8, span_x), F32),
        pltpu.VMEM((2, 8, span_x), F32),
        pltpu.VMEM((ny, 2, 8, span_x), F32),
        pltpu.SemaphoreType.DMA((4, 8)),
        pltpu.SemaphoreType.DMA((4, 8)),
        pltpu.SemaphoreType.DMA((nz,)),
        pltpu.SemaphoreType.DMA((nz,)),
        pltpu.SemaphoreType.DMA((ny,)),
        pltpu.SemaphoreType.DMA((ny,)),
    ]
    outs = pl.pallas_call(
        functools.partial(kernel, ny, nz, span_y, span_z, span_x, rows, chunk),
        out_shape=(
            shape((3, rows), F32), shape((3, rows), F32), shape((9, rows), F32), shape((9, rows), F32),
            shape((2, 8, span_x), F32),
        ),
        in_specs=[vmem, vmem, vmem, vmem, vmem, smem, vmem, smem, vmem, vmem, vmem, vmem],
        out_specs=(vmem,) * 5,
        scratch_shapes=scratch,
        compiler_params=pltpu.CompilerParams(
            collective_id=0, has_side_effects=True, vmem_limit_bytes=56 * 1024 * 1024
        ),
    )(offset, velocity, affine, deform, cell_index.reshape(1, rows), live_count, grip_mask,
      grip_velocity.reshape(-1), loss_offset, loss_velocity, loss_affine, loss_deform)
    grad_grip = outs[4][:, :6, 0].reshape(2, 2, 3)
    return (outs[0], outs[1], outs[2], outs[3], grad_grip)


def solution(mesh):
    rows = P(None, ("gy", "gz"))
    ny, nz = mesh.shape["gy"], mesh.shape["gz"]
    return jax.shard_map(
        functools.partial(shards, ny, nz),
        mesh=mesh,
        in_specs=(
            rows, rows, rows, rows, P(("gy", "gz")), P(("gy", "gz")), P("gy", "gz", None), P(),
            rows, rows, rows, rows,
        ),
        out_specs=(rows, rows, rows, rows, P()),
        check_vma=False,
    )
```

profile of v0, /device:TPU:0, one launch (start us, length us, event | category | flops | bytes accessed | tf_op | source)
XLA Modules:
  0.0 100.2 jit_solution(14661910023414072456)
XLA Ops:
  0.6 0.0 copy-start.2
  1.3 0.0 copy-done.2
  1.3 0.6 reshape.17.grip_ref
  1.9 92.4 %shard_map.155 = (f32[3,2048]{1,0:T(4,128)}, f32[3,2048]{1,0:T(4,128)}, f32[9,2048]{1,0:T(8,128)}, f32[9,2048]{1,0:T(8,128)}, f32[2,8,128]{2,1,0:T(8,128)}) custom-call(f32[3,2048]{1,0:T(4,128)} %off_ref.1, f32[3,2048]{1,0:T(4,128)} %vel_ref.1, f32[9,2048]{1,0:T(8,128)} %aff_ref.1, f32[9,2048]{1,0:T(8,128)} %def_ref.1, s32[1,2048]{1,0:T(1,128)} %bitcast.1, ...), custom_call_target="tpu_custom_call" | custom-call | tf_op jit(solution)/shard_map/pallas_call | solution.py:584
  94.3 0.0 copy-start.1
  94.3 0.8 slice_reduce_fusion
  95.2 0.7 reshape_squeeze.3
  95.8 1.4 %copy.22 = f32[3,2048]{1,0:T(4,128)} copy(f32[3,2048]{1,0:T(4,128)} %get-tuple-element.20) | data formatting | bytes 49152
  97.2 1.4 %copy.23 = f32[3,2048]{1,0:T(4,128)} copy(f32[3,2048]{1,0:T(4,128)} %get-tuple-element.21) | data formatting | bytes 49152
  98.6 0.0 copy-done.1
  98.6 0.0 copy-start
  98.6 0.7 copy.24
  99.2 0.3 copy-done
  99.5 0.7 copy.25
Async XLA Ops:
  0.6 0.7 copy-start.2
  94.3 4.3 %copy-start.1 = (f32[9,2048]{1,0:T(8,128)S(1)}, f32[9,2048]{1,0:T(8,128)}, u32[]{:S(2)}) copy-start(f32[9,2048]{1,0:T(8,128)} %get-tuple-element.22) | copy-start | bytes 221188
  98.6 1.0 copy-start
where the time goes:
time: 101 us; the launch traced here: 100 us
  Pallas kernels  92.4 us (91%)
  local copies, waits for them, and re-layouts  6.45 us (6%)
  between operations  1.32 us (1%)
    pallas_call x1, Pallas kernels, shards(): pl.pallas_call(functools.partial(kernel, ny, nz, span_y, span_z, span_x,...  92.4 us
    unnamed x10, local copies, waits for them, and re-layouts  4.38 us

commit v1 on v0

--- a/solution.py
+++ b/solution.py
@@ -179,13 +179,10 @@
                 his.append(hi)
                 los.append(lo)
         hot = oht[sl, :]
-        for i in range(4 if mass else 3):
-            hi = jnp.concatenate(his[3 * i:3 * i + 3], axis=0)
-            lo = jnp.concatenate(los[3 * i:3 * i + 3], axis=0)
-            part = jnp.dot(hi, hot, preferred_element_type=F32)
-            part = part + jnp.dot(lo, hot, preferred_element_type=F32)
-            height = 3 * zr * 8
-            acc[i * height:(i + 1) * height, :] += part
+        total = (12 if mass else 9) * zr * 8
+        part = jnp.dot(jnp.concatenate(his, axis=0), hot, preferred_element_type=F32)
+        part = part + jnp.dot(jnp.concatenate(los, axis=0), hot, preferred_element_type=F32)
+        acc[0:total, :] += part
 
     def fold(comps):
         for i in range(comps):
@@ -310,11 +307,13 @@
         hot = oh[:, sl]
         bits = [(pz & (1 << k)) != 0 for k in range(zbits)]
         out = []
+        total = 3 * comps * zr * 8
+        every = jnp.dot(u_hi[0:total, :], hot, preferred_element_type=F32)
+        every = every + jnp.dot(u_lo[0:total, :], hot, preferred_element_type=F32)
         for i in range(comps):
             for a in range(3):
                 at = (3 * i + a) * zr * 8
-                h = jnp.dot(u_hi[at:at + zr * 8, :], hot, preferred_element_type=F32)
-                h = h + jnp.dot(u_lo[at:at + zr * 8, :], hot, preferred_element_type=F32)
+                h = every[at:at + zr * 8]
                 vals = [h[z * 8:(z + 1) * 8] for z in range(zr)]
                 for k in reversed(range(zbits)):
                     shift = 1 << k
@@ -537,7 +536,7 @@
            loss_offset, loss_velocity, loss_affine, loss_deform):
     span_y, span_z, span_x = grip_mask.shape
     rows = offset.shape[1]
-    chunk = 256
+    chunk = 1024
     zr = span_z + 2
     bands = span_y // YB
     yp = (span_y + 2 + 7) // 8 * 8

time: 101 us -> 81.8 us (0.81)
  Pallas kernels: 92.4 us -> 73.7 us
    pallas_call x1, Pallas kernels: 92.4 us -> 73.7 us  [shards(): pl.pallas_call(functools.partial(kernel, ny, nz, span_y, span_z, span_x,...]
where the time goes in v1:
time: 81.8 us; the launch traced here: 81.5 us
  Pallas kernels  73.7 us (90%)
  local copies, waits for them, and re-layouts  6.45 us (8%)
  between operations  1.32 us (2%)
    pallas_call x1, Pallas kernels, shards(): pl.pallas_call(functools.partial(kernel, ny, nz, span_y, span_z, span_x,...  73.7 us
    unnamed x10, local copies, waits for them, and re-layouts  4.38 us

profile of v1, /device:TPU:0, one launch (start us, length us, event | category | flops | bytes accessed | tf_op | source)
XLA Modules:
  0.0 81.5 jit_solution(2972965397349754798)
XLA Ops:
  0.6 0.0 copy-start.2
  1.3 0.0 copy-done.2
  1.3 0.6 reshape.17.grip_ref
  1.9 73.7 %shard_map.155 = (f32[3,2048]{1,0:T(4,128)}, f32[3,2048]{1,0:T(4,128)}, f32[9,2048]{1,0:T(8,128)}, f32[9,2048]{1,0:T(8,128)}, f32[2,8,128]{2,1,0:T(8,128)}) custom-call(f32[3,2048]{1,0:T(4,128)} %off_ref.1, f32[3,2048]{1,0:T(4,128)} %vel_ref.1, f32[9,2048]{1,0:T(8,128)} %aff_ref.1, f32[9,2048]{1,0:T(8,128)} %def_ref.1, s32[1,2048]{1,0:T(1,128)} %bitcast.1, ...), custom_call_target="tpu_custom_call" | custom-call | tf_op jit(solution)/shard_map/pallas_call | solution.py:583
  75.7 0.0 copy-start.1
  75.7 0.8 %slice_reduce_fusion = f32[2,6]{1,0:T(2,128)S(1)} fusion(f32[2,8,128]{2,1,0:T(8,128)} %get-tuple-element.14), kind=kLoop, calls=%fused_computation | loop fusion | bytes 96 | tf_op jit(solution)/shard_map/slice | solution.py:597
  76.5 0.7 reshape_squeeze.3
  77.1 1.4 %copy.22 = f32[3,2048]{1,0:T(4,128)} copy(f32[3,2048]{1,0:T(4,128)} %get-tuple-element.20) | data formatting | bytes 49152
  78.5 1.4 %copy.23 = f32[3,2048]{1,0:T(4,128)} copy(f32[3,2048]{1,0:T(4,128)} %get-tuple-element.21) | data formatting | bytes 49152
  79.9 0.0 copy-done.1
  79.9 0.0 copy-start
  79.9 0.7 copy.24
  80.6 0.3 copy-done
  80.9 0.7 copy.25
Async XLA Ops:
  0.6 0.7 copy-start.2
  75.7 4.3 %copy-start.1 = (f32[9,2048]{1,0:T(8,128)S(1)}, f32[9,2048]{1,0:T(8,128)}, u32[]{:S(2)}) copy-start(f32[9,2048]{1,0:T(8,128)} %get-tuple-element.22) | copy-start | bytes 221188
  79.9 1.0 %copy-start = (f32[9,2048]{1,0:T(8,128)S(1)}, f32[9,2048]{1,0:T(8,128)}, u32[]{:S(2)}) copy-start(f32[9,2048]{1,0:T(8,128)} %get-tuple-element.23) | copy-start | bytes 221188

commit v2 on v1

--- a/solution.py
+++ b/solution.py
@@ -127,14 +127,19 @@
         sl = pl.ds(pl.multiple_of(s * chunk, chunk), chunk)
         col = column(sl)
         wide = bands * span_x
-        rows_iota = lax.broadcasted_iota(jnp.int32, (wide, chunk), 0)
-        oh[:, sl] = jnp.where(rows_iota == col, 1.0, 0.0).astype(BF16)
         col_t = jnp.transpose(jnp.broadcast_to(col.astype(F32), (128, chunk)))
         lane = lax.broadcasted_iota(jnp.int32, (chunk, 128), 1)
         for part in range(wide // 128):
             oht[sl, part * 128:(part + 1) * 128] = jnp.where(
                 col_t == (lane + part * 128).astype(F32), 1.0, 0.0
             ).astype(BF16)
+
+    def build_oh():
+        @pl.loop(0, steps)
+        def _(s):
+            sl = pl.ds(pl.multiple_of(s * chunk, chunk), chunk)
+            rows_iota = lax.broadcasted_iota(jnp.int32, (bands * span_x, chunk), 0)
+            oh[:, sl] = jnp.where(rows_iota == column(sl), 1.0, 0.0).astype(BF16)
 
     def geometry(sl):
         rem = idx_ref[:, sl] >> xbits
@@ -220,7 +225,7 @@
             return ry.at[e, 0 if dy < 0 else 1, pl.ds(0, n)]
         return rc.at[e, (0 if dy < 0 else 2) + (0 if dz < 0 else 1), pl.ds(0, n)]
 
-    def exchange(e, out):
+    def exchange(e, out, during):
         n = COMPS[e]
         ybuf[0, 0:n] = grid[0:n, :, 0:2, :]
         ybuf[1, 0:n] = grid[0:n, :, span_y:span_y + 2, :]
@@ -235,6 +240,7 @@
                 ).start()
         for i in range(n):
             out(i)[...] = grid[i]
+        during()
         for d in order:
             dy, dz = DIRS[d]
 
@@ -383,7 +389,7 @@
             for z in range(span_z):
                 grid[4, z + 1, 1:span_y + 1, :] = mask_ref[:, z, :].astype(F32)
             barrier_wait()
-        exchange(e, lambda i: sums.at[e, i] if i < 4 else maskx)
+        exchange(e, lambda i: sums.at[e, i] if i < 4 else maskx, build_oh if e == 0 else nothing)
         settle(e)
         n_o, n_v, n_a, n_d = afters[e]
 
@@ -439,18 +445,13 @@
             scatter_chunk(s, sl, row_list(o_r, sl), g, d_mat, None, False)
 
         fold(3)
-        exchange(3 - e, lambda i: sums.at[2, i])
-        settle_back(e)
-        before()
         outs = (up_o, up_v, up_a, up_d) if e == 1 else (go_ref, gv_ref, ga_ref, gd_ref)
 
-        def body(s):
+        def through_gather(s):
             sl = pl.ds(pl.multiple_of(s * chunk, chunk), chunk)
             _, b = geometry(sl)
-            live = live_of(s)
             f = row_list(o_r, sl)
-            dm = row_list(d_r, sl)
-            g_o, g_d, g, d_mat = gather_seeds(e, s, sl, dm)
+            g_o, g_d, g, d_mat = gather_seeds(e, s, sl, row_list(d_r, sl))
             held = [[node[e, 3 * r + c, :, sl] for c in range(3)] for r in range(9)]
             pull = weight_pull(held, f, b, g, d_mat, False)
             vn = row_list(n_v, sl)
@@ -463,6 +464,23 @@
                 for j in range(3)
                 for k in range(3)
             ]
+            for k in range(3):
+                outs[0][k:k + 1, sl] = grad_o[k]
+            for k in range(9):
+                outs[3][k:k + 1, sl] = grad_d[k]
+
+        exchange(3 - e, lambda i: sums.at[2, i], lambda: pl.loop(0, steps)(through_gather))
+        settle_back(e)
+        before()
+
+        def body(s):
+            sl = pl.ds(pl.multiple_of(s * chunk, chunk), chunk)
+            _, b = geometry(sl)
+            live = live_of(s)
+            f = row_list(o_r, sl)
+            dm = row_list(d_r, sl)
+            grad_o = row_list(outs[0], sl)
+            grad_d = row_list(outs[3], sl)
             vals = gather_chunk(sl, 4)
             plain, first = moments(vals, f, b)
             grad_v = [live * m for m in plain]

time: 81.8 us -> 79.9 us (0.977)
  Pallas kernels: 73.7 us -> 71.8 us
    pallas_call x1, Pallas kernels: 73.7 us -> 71.8 us  [shards(): pl.pallas_call(functools.partial(kernel, ny, nz, span_y, span_z, span_x,...]
where the time goes in v2:
time: 79.9 us; the launch traced here: 79.6 us
  Pallas kernels  71.8 us (90%)
  local copies, waits for them, and re-layouts  6.45 us (8%)
  between operations  1.32 us (2%)
    pallas_call x1, Pallas kernels, shards(): pl.pallas_call(functools.partial(kernel, ny, nz, span_y, span_z, span_x,...  71.8 us
    unnamed x10, local copies, waits for them, and re-layouts  4.38 us

profile of v2, /device:TPU:0, one launch (start us, length us, event | category | flops | bytes accessed | tf_op | source)
XLA Modules:
  0.0 79.6 jit_solution(5853577123371965036)
XLA Ops:
  0.6 0.0 copy-start.2
  1.3 0.0 copy-done.2
  1.3 0.6 reshape.17.grip_ref
  1.9 71.8 %shard_map.155 = (f32[3,2048]{1,0:T(4,128)}, f32[3,2048]{1,0:T(4,128)}, f32[9,2048]{1,0:T(8,128)}, f32[9,2048]{1,0:T(8,128)}, f32[2,8,128]{2,1,0:T(8,128)}) custom-call(f32[3,2048]{1,0:T(4,128)} %off_ref.1, f32[3,2048]{1,0:T(4,128)} %vel_ref.1, f32[9,2048]{1,0:T(8,128)} %aff_ref.1, f32[9,2048]{1,0:T(8,128)} %def_ref.1, s32[1,2048]{1,0:T(1,128)} %bitcast.1, ...), custom_call_target="tpu_custom_call" | custom-call | tf_op jit(solution)/shard_map/pallas_call | solution.py:601
  73.7 0.0 copy-start.1
  73.7 0.8 %slice_reduce_fusion = f32[2,6]{1,0:T(2,128)S(1)} fusion(f32[2,8,128]{2,1,0:T(8,128)} %get-tuple-element.14), kind=kLoop, calls=%fused_computation | loop fusion | bytes 96 | tf_op jit(solution)/shard_map/slice | solution.py:615
  74.5 0.7 reshape_squeeze.3
  75.2 1.4 %copy.22 = f32[3,2048]{1,0:T(4,128)} copy(f32[3,2048]{1,0:T(4,128)} %get-tuple-element.20) | data formatting | bytes 49152
  76.6 1.4 %copy.23 = f32[3,2048]{1,0:T(4,128)} copy(f32[3,2048]{1,0:T(4,128)} %get-tuple-element.21) | data formatting | bytes 49152
  78.0 0.0 copy-done.1
  78.0 0.0 copy-start
  78.0 0.7 copy.24
  78.6 0.3 copy-done
  78.9 0.7 copy.25
Async XLA Ops:
  0.6 0.7 copy-start.2
  73.7 4.3 %copy-start.1 = (f32[9,2048]{1,0:T(8,128)S(1)}, f32[9,2048]{1,0:T(8,128)}, u32[]{:S(2)}) copy-start(f32[9,2048]{1,0:T(8,128)} %get-tuple-element.22) | copy-start | bytes 221188
  78.0 1.0 %copy-start = (f32[9,2048]{1,0:T(8,128)S(1)}, f32[9,2048]{1,0:T(8,128)}, u32[]{:S(2)}) copy-start(f32[9,2048]{1,0:T(8,128)} %get-tuple-element.23) | copy-start | bytes 221188
